TPU v7x, 32 devices: a whole 2x2x4 slice. The times are simulated.
32 devices in a mesh: member: 2 (over x), sub: 8 (over z, y), var: 2 (over core).
Axes of the slice: x: 2, y: 2, z: 4, core: 2. Of those that a mesh axis runs over, the one named last changes fastest.
Arguments:
- innovations: float32 [8, 65536], P('var', ('member', 'sub')), parts along dimension 1, may hold values from -6 to 6
- obs_owner: int32 [65536, 1], P(('member', 'sub')), parts along dimension 0, may hold values from 0 to 7; in each aligned block of 4096 rows (0 to 4095, 4096 to 8191, ...) at most 1024 rows name the same one
- obs_local: int32 [65536], P(('member', 'sub')), parts along dimension 0, may hold values from 0 to 2047
- obs_level: int32 [65536, 1], P(('member', 'sub')), parts along dimension 0, may hold values from 0 to 63; in each aligned block of 4096 rows (0 to 4095, 4096 to 8191, ...) at most 128 rows name the same one
- band_width: int32 [64], replicated, may hold values from 2 to 16
- vert_scale: float32 [8, 64], P('var'), may hold values from 1 to 4
- sigma: float32 [8, 64], P('var'), may hold values from 0.5 to 2
- balance: float32 [8, 8], P('var')
Outputs:
- increment: float32 [8, 64, 64, 512], P('var', None, ('member', 'sub')), parts along dimension 2
There are 2 independent parts, one for each index of `member`. A program takes and returns all parts, laid end to end along the dimension named above; an argument that names none is the same for every part. Nothing has to cross between parts.
Inputs may be any that keep to these rules, and one draw needn't show every extreme that they name: `obs_owner`: in the rows of one device no subdomain is named more than 1024 times, a bound that some block reaches. `obs_level`: in the rows of one device no level is named more than 128 times, a bound that some block reaches.
All inputs are finite; a program needn't handle non-finite values.
Results may differ from a plain program's by a relative error of at most 0.00008.
Values sent between devices are 32-bit elements; how exact they have to be, the bound alone decides.
A program may use at most 192 MiB of HBM per device.

v0:
```python
import jax
import jax.numpy as jnp
from jax import lax
from jax.sharding import PartitionSpec as P

VB = 6
NX_DEV = 4
NY = 512


def filter_matrix(width, count):
    rate = width.astype(jnp.float32)[:, None, None]
    index = jnp.arange(count)
    dist = jnp.abs(index[:, None] - index[None, :]).astype(jnp.float32)
    far = (count - jnp.maximum(index[:, None], index[None, :])).astype(jnp.float32)
    return jnp.exp(-dist / rate) * (1.0 - jnp.exp(-2.0 * far / rate))


def vertical_matrix(scale, levels):
    index = jnp.arange(levels)
    dist = (index[:, None] - index[None, :]).astype(jnp.float32)
    corr = jnp.exp(-dist * dist / (2.0 * scale[:, :, None] * scale[:, None, :]))
    return jnp.where(jnp.abs(dist) <= VB, corr, jnp.float32(0.0))


def smooth(field, across, along):
    high = lax.Precision.HIGHEST
    part = jnp.einsum("lij,vljy->vliy", across, field, precision=high)
    return jnp.einsum("vlxj,lyj->vlxy", part, along, precision=high)


def slot_rank(target, count):
    hits = (target[:, None] == jnp.arange(count)[None, :]).astype(jnp.int32)
    return jnp.sum((jnp.cumsum(hits, 0) - hits) * hits, 1)


def on_device(innovations, obs_owner, obs_local, obs_level, band_width, vert_scale, sigma, balance):
    groups = lax.axis_size("sub")
    here = lax.axis_index("sub")
    nvar, nobs = innovations.shape
    levels = band_width.shape[0]
    depth = levels // groups
    wide = NX_DEV * groups
    mine = lax.dynamic_slice_in_dim(band_width, here * depth, depth)
    across = filter_matrix(mine, wide)
    along = filter_matrix(mine, NY)
    owner = obs_owner[:, 0]
    level = obs_level[:, 0]
    limit = 2 * nobs // groups
    target = owner * limit + slot_rank(owner, groups)
    place = level * (NX_DEV * NY) + obs_local
    values = jnp.zeros((nvar, groups * limit), jnp.float32).at[:, target].set(innovations)
    spots = jnp.zeros((groups * limit,), jnp.int32).at[target].set(place)
    values, spots = (
        lax.all_to_all(
            values.reshape(nvar, groups, limit), "sub", split_axis=1, concat_axis=1, tiled=True
        ),
        lax.all_to_all(
            spots.reshape(1, groups, limit), "sub", split_axis=1, concat_axis=1, tiled=True
        ),
    )
    column = jnp.zeros((nvar, levels * NX_DEV * NY), jnp.float32)
    column = column.at[:, spots.reshape(-1)].add(values.reshape(nvar, -1))
    column = column.reshape(nvar, levels, NX_DEV, NY)
    slab = smooth(
        lax.all_to_all(column, "sub", split_axis=1, concat_axis=2, tiled=True), across, along
    )
    corr = vertical_matrix(vert_scale, levels)
    correlated = jnp.einsum(
        "vlm,vmxy->vlxy",
        corr,
        lax.all_to_all(slab, "sub", split_axis=2, concat_axis=1, tiled=True),
        precision=lax.Precision.HIGHEST,
    )
    mixed = jnp.einsum(
        "vu,ulxy->vlxy",
        balance,
        lax.all_gather(correlated, "var", axis=0, tiled=True),
        precision=lax.Precision.HIGHEST,
    )
    return mixed * sigma[:, :, None, None]


def solution(mesh):
    in_specs = (
        P("var", ("member", "sub")),
        P(("member", "sub"), None),
        P(("member", "sub")),
        P(("member", "sub"), None),
        P(),
        P("var", None),
        P("var", None),
        P("var", None),
    )
    out_specs = P("var", None, ("member", "sub"), None)
    return jax.shard_map(
        on_device, mesh=mesh, in_specs=in_specs, out_specs=out_specs, check_vma=False
    )
```

profile of v0, /device:TPU:0, one launch (start us, length us, event | category | flops | bytes accessed | tf_op | source)
XLA Modules:
  0.0 395.1 jit_solution(10532747100811612458)
XLA Ops:
  6.5 0.0 copy-start
  6.5 0.7 fusion.44
  7.3 2.3 reduce-window.6
  9.6 0.3 slice_reduce_fusion
  9.9 0.2 reduce-window.9
  10.1 0.1 add_bitcast_fusion
  10.2 0.8 fusion.38
  11.0 0.7 compare_select_fusion.1
  11.8 0.7 broadcast_multiply_fusion
  12.5 0.7 add.33
  13.2 16.1 %scatter_custom_fusion = s32[8192]{0:T(1024)} fusion(s32[4096]{0:T(1024)S(1)} %bitcast.89, s32[4096]{0:T(1024)S(1)} %add.33, s32[]{:T(128)} %constant.22.clone.1), kind=kCustom, calls=%fused_computation.68 | custom fusion | bytes 32772 | tf_op jit(solution)/shard_map/scatter | solution.py:53
  29.3 7.3 %all-to-all-start = ((s32[1,8,1024]{2,0,1:T(1,128)}), s32[1,8,1024]{2,0,1:T(1,128)S(1)}, u32[]{:S(2)}, u32[]{:S(2)}) async-start(s32[1,8,1024]{2,0,1:T(1,128)} %bitcast.10), calls=%async_computation | async-start | bytes 65536 | tf_op jit(solution)/shard_map/all_to_all | solution.py:58
  36.6 1.5 copy.34
  38.1 12.8 %scatter_custom_fusion.1 = f32[4,8192]{0,1:T(8,128)} fusion(s32[4096]{0:T(1024)S(1)} %bitcast.90, f32[4096,4]{1,0:T(8,128)S(1)} %copy.34, f32[]{:T(128)} %constant.18.clone.1), kind=kCustom, calls=%fused_computation.27 | custom fusion | bytes 131076 | tf_op jit(solution)/shard_map/scatter | solution.py:52
  50.8 3.5 copy.35
  54.3 0.0 all-to-all-done
  54.3 6.5 %all-to-all-start.1 = ((f32[4,8,1024]{2,0,1:T(4,128)}), f32[4,8,1024]{2,0,1:T(4,128)S(1)}, u32[]{:S(2)}, u32[]{:S(2)}) async-start(f32[4,8,1024]{2,0,1:T(4,128)} %copy.35), calls=%async_computation.1 | async-start | bytes 262144 | tf_op jit(solution)/shard_map/all_to_all | solution.py:55
  60.9 5.9 %sort = (s32[8192]{0:T(1024)S(1)}, s32[8192]{0:T(1024)S(1)}) sort(s32[8192]{0:T(1024)S(1)} %bitcast.84, s32[8192]{0:T(1024)S(1)} %iota.70), dimensions={0}, to_apply=%compare | sort | flops 106496 | bytes 131072 | tf_op jit(solution)/shard_map/scatter-add | solution.py:63
  66.8 1.3 all-to-all-done.1
  68.1 2.6 copy.36
  70.8 121.5 %scatter_custom_fusion.2 = f32[4,131072]{0,1:T(8,128)} fusion(s32[8192]{0:T(1024)S(1)} %get-tuple-element.5, f32[]{:T(128)} %constant.18.clone.1, f32[8192,4]{1,0:T(8,128)} %copy.36, s32[8192]{0:T(1024)S(1)} %broadcast_clamp_fusion), kind=kCustom, calls=%fused_computation.4 | custom fusion | flops 32768 | bytes 2097664 | tf_op jit(solution)/shard_map/scatter-add | solution.py:63
  192.2 35.3 %copy.37 = f32[4,64,4,512]{3,2,0,1:T(4,128)} copy(f32[4,64,4,512]{0,3,2,1:T(8,128)} %bitcast.17) | data formatting | bytes 4194304 | tf_op jit(solution)/shard_map/reshape | solution.py:64
  227.5 0.0 copy-start.4
  227.5 16.3 %all-to-all-start.2 = ((f32[4,64,4,512]{3,2,0,1:T(4,128)}), f32[4,64,4,512]{3,2,0,1:T(4,128)S(1)}, u32[]{:S(2)}, u32[]{:S(2)}) async-start(f32[4,64,4,512]{3,2,0,1:T(4,128)} %copy.37), calls=%async_computation.2 | async-start | bytes 4194304 | tf_op jit(solution)/shard_map/all_to_all | solution.py:66
  243.8 0.0 copy-done.4
  243.8 0.1 dynamic-slice_convert_fusion
  243.9 1.3 convert_multiply_fusion
  245.2 45.3 %all-to-all-done.2 = f32[4,64,4,512]{3,2,0,1:T(4,128)S(1)} async-done(((f32[4,64,4,512]{3,2,0,1:T(4,128)}), f32[4,64,4,512]{3,2,0,1:T(4,128)S(1)}, u32[]{:S(2)}, u32[]{:S(2)}) %all-to-all-start.2) | async-done | bytes 2097184 | tf_op jit(solution)/shard_map/all_to_all | solution.py:66
  290.5 1.2 copy.64
  291.8 0.0 copy-start.1
  291.8 0.2 copy.39
  292.0 3.7 fusion.21
  295.7 0.0 copy-done.1
  295.7 11.0 %fusion.27 = f32[4,8,32,512]{3,2,0,1:T(8,128)S(1)} fusion(f32[8,4,512,32]{2,3,1,0:T(8,128)S(1)} %fusion.21, f32[512,512]{1,0:T(8,128)S(1)} %get-tuple-element.9, f32[8]{0:T(128)S(1)} %dynamic-slice_convert_fusion, f32[512,512]{1,0:T(8,128)S(1)} %copy-done.1), kind=kOutput, calls=%fused_computation.29 | convolution fusion | flops 3229614080 | bytes 6291488 | tf_op jit(solution)/shard_map/vlxj,lyj->vlxy/dot_general | solution.py:29
  306.8 0.0 copy-start.2
  306.8 2.7 copy.41
  309.4 3.6 all-to-all-start.3
  313.1 0.0 all-gather.2.cloned.1.call-start
  313.1 0.0 copy-done.2
  313.2 48.3 %all-to-all-done.3 = f32[4,8,32,512]{3,0,1,2:T(4,128)S(1)} async-done(((f32[4,8,32,512]{3,0,1,2:T(4,128)}), f32[4,8,32,512]{3,0,1,2:T(4,128)S(1)}, u32[]{:S(2)}, u32[]{:S(2)}) %all-to-all-start.3) | async-done | bytes 2097184 | tf_op jit(solution)/shard_map/all_to_all | solution.py:72
  361.5 0.7 copy.42
  362.2 0.0 copy-start.3
  362.2 3.3 fusion.17
  365.5 0.0 all-gather.2.cloned.1.call-update
  365.5 0.0 copy-done.3
  365.5 0.1 copy.45
  365.6 11.8 %all-gather.2.cloned.1.call-done = f32[8,64,4,512]{3,1,2,0:T(8,128)} async-done(((f32[4,64,4,512]{3,1,2,0:T(8,128)}), f32[8,64,4,512]{3,1,2,0:T(8,128)}) %all-gather.2.cloned.1.call-update) | async-done | bytes 4194320 | tf_op jit(solution)/shard_map/all_gather | solution.py:78
  377.4 0.0 copy-done
  377.4 8.5 %bitcast_multiply_fusion = f32[4,64,4,512]{3,0,2,1:T(4,128)S(1)} fusion(f32[8,64,4,512]{3,1,2,0:T(8,128)} %all-gather.2.cloned.1.call-done, f32[4,64]{0,1:T(8,128)S(1)} %copy.45, f32[4,8]{1,0:T(4,128)S(1)} %copy-done), kind=kOutput, calls=%fused_computation.19 | convolution fusion | flops 50855936 | bytes 6292608 | tf_op jit(solution)/shard_map/vu,ulxy->vlxy/dot_general | solution.py:75
  386.0 2.1 copy.46
  (7 shorter events, 0.1 us)
Async XLA Ops:
  6.5 370.9 %copy-start = (f32[4,8]{1,0:T(4,128)S(1)}, f32[4,8]{1,0:T(4,128)}, u32[]{:S(2)}) copy-start(f32[4,8]{1,0:T(4,128)} %param.15) | copy-start | bytes 388
  29.3 25.0 %all-to-all-start = ((s32[1,8,1024]{2,0,1:T(1,128)}), s32[1,8,1024]{2,0,1:T(1,128)S(1)}, u32[]{:S(2)}, u32[]{:S(2)}) async-start(s32[1,8,1024]{2,0,1:T(1,128)} %bitcast.10), calls=%async_computation | async-start | bytes 65536 | tf_op jit(solution)/shard_map/all_to_all | solution.py:58
  54.3 13.8 %all-to-all-start.1 = ((f32[4,8,1024]{2,0,1:T(4,128)}), f32[4,8,1024]{2,0,1:T(4,128)S(1)}, u32[]{:S(2)}, u32[]{:S(2)}) async-start(f32[4,8,1024]{2,0,1:T(4,128)} %copy.35), calls=%async_computation.1 | async-start | bytes 262144 | tf_op jit(solution)/shard_map/all_to_all | solution.py:55
  227.5 16.3 %copy-start.4 = (s32[64]{0:T(128)S(1)}, s32[64]{0:T(128)}, u32[]{:S(2)}) copy-start(s32[64]{0:T(128)} %param.12) | copy-start | bytes 772
  227.5 63.0 %all-to-all-start.2 = ((f32[4,64,4,512]{3,2,0,1:T(4,128)}), f32[4,64,4,512]{3,2,0,1:T(4,128)S(1)}, u32[]{:S(2)}, u32[]{:S(2)}) async-start(f32[4,64,4,512]{3,2,0,1:T(4,128)} %copy.37), calls=%async_computation.2 | async-start | bytes 4194304 | tf_op jit(solution)/shard_map/all_to_all | solution.py:66
  291.8 4.0 %copy-start.1 = (f32[512,512]{1,0:T(8,128)S(1)}, f32[512,512]{1,0:T(8,128)}, u32[]{:S(2)}) copy-start(f32[512,512]{1,0:T(8,128)} %get-tuple-element.10) | copy-start | bytes 3145732
  306.8 6.4 %copy-start.2 = (f32[4,64]{1,0:T(4,128)S(1)}, f32[4,64]{1,0:T(4,128)}, u32[]{:S(2)}) copy-start(f32[4,64]{1,0:T(4,128)} %param.13) | copy-start | bytes 3076
  309.4 52.1 %all-to-all-start.3 = ((f32[4,8,32,512]{3,0,1,2:T(4,128)}), f32[4,8,32,512]{3,0,1,2:T(4,128)S(1)}, u32[]{:S(2)}, u32[]{:S(2)}) async-start(f32[4,8,32,512]{3,0,1,2:T(4,128)} %copy.41), calls=%async_computation.3 | async-start | bytes 4194304 | tf_op jit(solution)/shard_map/all_to_all | solution.py:72
  313.1 64.4 %all-gather.2.cloned.1.call-start = ((), (), s32[]{:S(2)}) async-start(), calls=%async_computation.4 | async-start | bytes 6291456 | tf_op jit(solution)/shard_map/all_gather | solution.py:78
  362.2 3.3 copy-start.3
Sparse Core Ops, SparseCore 0:
  365.6 11.7 all-gather.1
where the time goes:
time: 400 us; the launch traced here: 395 us
  other arithmetic  135 us (34%)
  waiting for transfers between devices  107 us (27%)
  local copies, waits for them, and re-layouts  79.1 us (20%)
  starting transfers between devices  33.7 us (8%)
  matrix products  26.5 us (7%)
  between operations  13.8 us (3%)
    scatter-add x3, other arithmetic, on_device(): column = column.at[:, spots.reshape(-1)].add(values.reshape(nvar, -1))  127 us
    all_to_all x1, waiting for transfers between devices, on_device(): lax.all_to_all(slab, 'sub', split_axis=2, concat_axis=1, tiled=True)  48.3 us
    all_to_all x1, waiting for transfers between devices, on_device(): lax.all_to_all(column, 'sub', split_axis=1, concat_axis=2, tiled=True)  45.3 us
    reshape x1, local copies, waits for them, and re-layouts, on_device(): column = column.reshape(nvar, levels, NX_DEV, NY)  35.3 us
    all_to_all x1, starting transfers between devices, on_device(): lax.all_to_all(column, 'sub', split_axis=1, concat_axis=2, tiled=True)  16.3 us
    scatter x1, local copies, waits for them, and re-layouts, on_device(): spots = jnp.zeros((groups * limit,), jnp.int32).at[target].set(place)  16.1 us
    scatter x1, local copies, waits for them, and re-layouts, on_device(): jnp.zeros((nvar, groups * limit), jnp.float32).at[:, target]  12.8 us
    all_gather x1, waiting for transfers between devices, on_device(): lax.all_gather(correlated, 'var', axis=0, tiled=True)  11.8 us
  transfers between devices with their start and end apart: 5, of which 4 were waited for; matrix products, arithmetic and copies ran while one was open for 6% of the time, Pallas kernels for 0%

commit v1 on v0

v1 whole, which is shorter than its diff:
```python
import functools

import jax
import jax.numpy as jnp
from jax import lax
from jax.experimental import pallas as pl
from jax.experimental.pallas import tpu as pltpu
from jax.sharding import PartitionSpec as P

VB = 6
NX_DEV = 4
NY = 512
LCAP = 128
LANES = 128
BLOCKS = NY // LANES
TAPS = 2 * VB + 1
CHUNK = 8

NT = (((1,), (1,)), ((), ()))


def iota(shape, dim):
    return lax.broadcasted_iota(jnp.int32, shape, dim)


def split(x):
    high = x.astype(jnp.bfloat16)
    return high, (x - high.astype(jnp.float32)).astype(jnp.bfloat16)


def one_hot(count, value, width):
    number = iota((count, width), 0).astype(jnp.float32).astype(jnp.bfloat16)
    value = jnp.broadcast_to(value.astype(jnp.bfloat16), (count, width))
    return jnp.where(number == value, jnp.bfloat16(1), jnp.bfloat16(0))


def rank_own(levels, level_rows, spots, place):
    rows = level_rows.shape[0]
    lower = (iota((256, 256), 0) < iota((256, 256), 1)).astype(jnp.float32).astype(jnp.bfloat16)
    offset = jnp.zeros((levels, 1), jnp.float32)
    for at in range(0, rows, 2):
        level = jnp.concatenate([level_rows[at : at + 1, :], level_rows[at + 1 : at + 2, :]], axis=1)
        hits = (iota((levels, 256), 0) == level).astype(jnp.float32)
        before = jnp.dot(hits.astype(jnp.bfloat16), lower, preferred_element_type=jnp.float32)
        rank = jnp.sum(hits * (before + offset), axis=0, keepdims=True)
        offset = offset + jnp.sum(hits, axis=1, keepdims=True)
        slot = (level * LCAP + rank.astype(jnp.int32)) << 16
        place[at : at + 1, :] = slot[:, :LANES] + spots[at : at + 1, :]
        place[at + 1 : at + 2, :] = slot[:, LANES:] + spots[at + 1 : at + 2, :]


def bin_source(levels, table, bins, src, values, places, nvar):
    half = levels // 2
    rows = places.shape[1]
    per = 8
    for step in range(rows // per):
        lefts, rights = [], []
        for pair in range(per // 2):
            at = step * per + 2 * pair
            place = jnp.concatenate(
                [places[src, at : at + 1, :], places[src, at + 1 : at + 2, :]], axis=1
            )
            slot = place >> 16
            spot = place & 65535
            rights.append(
                one_hot(2 * LCAP, (slot & (2 * LCAP - 1)).astype(jnp.float32), 256)
            )
            pick = one_hot(half, (slot >> 8).astype(jnp.float32), 256)
            parts = []
            for v in range(nvar):
                parts += split(values[src, v : v + 1, at * LANES : (at + 2) * LANES])
            parts += [
                (spot >> 8).astype(jnp.float32).astype(jnp.bfloat16),
                (spot & 255).astype(jnp.float32).astype(jnp.bfloat16),
            ]
            lefts.append(jnp.concatenate([pick * part for part in parts], axis=0))
        left = jnp.concatenate(lefts, axis=1)
        right = jnp.concatenate(rights, axis=1)
        part = lax.dot_general(left, right, NT, preferred_element_type=jnp.float32)
        if step == 0:
            table[...] = part
        else:
            table[...] += part
    for parity in range(2):
        lanes = slice(parity * LCAP, (parity + 1) * LCAP)
        for v in range(nvar):
            at = 2 * v * half
            bins[src, parity, v] = (
                table[at : at + half, lanes] + table[at + half : at + 2 * half, lanes]
            )
        at = 2 * nvar * half
        spot = table[at : at + half, lanes] * 256.0 + table[at + half : at + 2 * half, lanes]
        spot = spot.astype(jnp.int32)
        bins[src, parity, nvar] = (spot >> 9).astype(jnp.float32)
        bins[src, parity, nvar + 1] = ((spot >> 7) & 3).astype(jnp.float32)
        bins[src, parity, nvar + 2] = (spot & 127).astype(jnp.float32)


def rate_of(band):
    return 1.0 / jnp.full((1, LANES), band.astype(jnp.float32), jnp.float32)


def add_level(groups, nvar, bins, pair, parity, rate, here):
    rows = nvar * NX_DEV
    wide = NX_DEV * groups
    near = (iota((8, LANES), 0) % NX_DEV + NX_DEV * here).astype(jnp.float32)
    which = iota((rows, LANES), 0) // NX_DEV
    total = None
    for first in range(0, groups, 8):
        lefts, rights = [], []
        for src in range(first, min(first + 8, groups)):
            def row(c):
                return bins[src, parity, c, pl.ds(pair, 1), :]

            x = row(nvar)
            gain = jnp.exp(-jnp.abs(near - x) * rate) * (
                1.0 - jnp.exp((-2.0 * rate) * (wide - jnp.maximum(near, x)))
            )
            gain = jnp.concatenate([gain] * (rows // 8), axis=0)
            value = row(nvar - 1)
            for v in range(nvar - 1):
                value = jnp.where(which == v, row(v), value)
            high, low = split(value * gain)
            block = jnp.broadcast_to(row(nvar + 1).astype(jnp.bfloat16), (rows, LANES))
            lefts.append(
                jnp.concatenate(
                    [
                        jnp.where(block == jnp.bfloat16(b), part, jnp.bfloat16(0))
                        for part in (high, low)
                        for b in range(BLOCKS)
                    ],
                    axis=0,
                )
            )
            rights.append(one_hot(LANES, row(nvar + 2), LANES))
        part = lax.dot_general(
            jnp.concatenate(lefts, axis=1),
            jnp.concatenate(rights, axis=1),
            NT,
            preferred_element_type=jnp.float32,
        )
        total = part if total is None else total + part
    size = BLOCKS * rows
    return total[:size] + total[size:]


def near_filter(rate):
    dist = jnp.abs(iota((LANES, LANES), 0) - iota((LANES, LANES), 1)).astype(jnp.float32)
    return jnp.concatenate(split(jnp.exp(-dist * rate)), axis=1)


def filter_level(nvar, total, near, rate, fields, level):
    rows = nvar * NX_DEV
    size = BLOCKS * rows
    quad = jnp.dot(
        jnp.concatenate(split(total), axis=0), near, preferred_element_type=jnp.float32
    )
    local = quad[:size, :LANES] + (quad[size:, :LANES] + quad[:size, LANES:])
    lane = iota((1, LANES), 1).astype(jnp.float32)
    to_end = jnp.exp((lane - (LANES - 1.0)) * rate)
    to_start = jnp.exp(-lane * rate)
    from_start = jnp.exp(-(lane + 1.0) * rate)
    from_end = jnp.exp((lane - float(LANES)) * rate)
    step = jnp.exp(-float(LANES) * rate)
    up = jnp.sum(total * to_end, axis=1, keepdims=True)
    down = jnp.sum(total * to_start, axis=1, keepdims=True)
    ups = [up[b * rows : (b + 1) * rows] for b in range(BLOCKS)]
    downs = [down[b * rows : (b + 1) * rows] for b in range(BLOCKS)]
    carry = [None] * BLOCKS
    for b in range(1, BLOCKS):
        carry[b] = ups[b - 1] if b == 1 else carry[b - 1] * step + ups[b - 1]
    edge = (carry[BLOCKS - 1] * step + ups[BLOCKS - 1]) * jnp.exp(-rate)
    back = [None] * BLOCKS
    back[BLOCKS - 1] = -edge
    for b in range(BLOCKS - 2, -1, -1):
        back[b] = back[b + 1] * step + downs[b + 1]
    for b in range(BLOCKS):
        out = local[b * rows : (b + 1) * rows] + back[b] * from_end
        if carry[b] is not None:
            out = out + carry[b] * from_start
        for v in range(nvar):
            fields[v, level + VB, b * NX_DEV : (b + 1) * NX_DEV, :] = out[
                v * NX_DEV : (v + 1) * NX_DEV
            ]


def kernel(
    groups, levels, nvar, value_ref, owner_ref, local_ref, level_ref, band_ref, scale_ref,
    sigma_ref, balance_ref, out_ref, values, places, place, table, bins, sums, filters, fields,
    mine, theirs, taps_vmem, taps, vsend, vrecv, psend, precv, swap_send, swap_recv, own_sem,
):
    here = lax.axis_index("sub")
    me = lax.axis_index("var")
    mesh_id = pl.DeviceIdType.MESH
    ranks = groups // 2
    line, side = here // 2, lax.rem(here, 2)
    twin = 2 * line + 1 - side
    barrier = pltpu.get_barrier_semaphore()
    friends = [2 * lax.rem(line + step, ranks) + side for step in range(1, ranks)]
    for peer in friends + [twin]:
        pl.semaphore_signal(barrier, inc=1, device_id={"sub": peer}, device_id_type=mesh_id)
    pl.semaphore_signal(barrier, inc=1, device_id={"var": 1 - me}, device_id_type=mesh_id)

    span = NX_DEV * NY
    rank_own(levels, level_ref, owner_ref[...] * span + local_ref[...], place)
    pl.semaphore_wait(barrier, ranks + 1)

    def send(slot, to, value_src, place_src):
        pair = []
        for source, target, out_sem, in_sem in (
            (value_src, values, vsend, vrecv), (place_src, places, psend, precv),
        ):
            copy = pltpu.make_async_remote_copy(
                src_ref=source, dst_ref=target.at[slot], send_sem=out_sem.at[slot],
                recv_sem=in_sem.at[slot], device_id={"sub": to}, device_id_type=mesh_id,
            )
            copy.start()
            pair.append(copy)
        return pair

    copies = {1: send(1, twin, value_ref, place)}
    for k, peer in enumerate(friends):
        copies[2 * k + 2] = send(2 * k + 2, peer, value_ref, place)
    own = [
        pltpu.make_async_copy(value_ref, values.at[0], own_sem.at[0]),
        pltpu.make_async_copy(place, places.at[0], own_sem.at[1]),
    ]
    for copy in own:
        copy.start()
    for copy in own:
        copy.wait()
    bin_source(levels, table, bins, 0, values, places, nvar)

    eye = iota((levels, levels), 0) == iota((levels, levels), 1)
    apart = (iota((levels, 2 * levels), 0) - iota((levels, 2 * levels), 1)).astype(jnp.float32)
    for v in range(nvar):
        across = scale_ref[v : v + 1, :]
        down = jnp.sum(jnp.where(eye, across, 0.0), axis=1, keepdims=True)
        across = jnp.concatenate([across, across], axis=1)
        taps_vmem[v * levels : (v + 1) * levels, :] = jnp.exp(
            -apart * apart / (2.0 * down * across)
        )
        fields[v, 0:VB] = jnp.zeros((VB,) + fields.shape[2:], jnp.float32)
        fields[v, VB + levels :] = jnp.zeros((VB,) + fields.shape[2:], jnp.float32)
    tap_copy = pltpu.make_async_copy(taps_vmem, taps, own_sem.at[2])
    tap_copy.start()

    def make_filter(quad, carry):
        for k in range(4):
            level = 4 * quad + k
            filters[level] = near_filter(rate_of(band_ref[level]))
        return carry

    lax.fori_loop(0, levels // 4, make_filter, 0)

    for k in range(1, ranks):
        for copy in copies[2 * k]:
            copy.wait_recv()
        copies[2 * k + 1] = send(2 * k + 1, twin, values.at[2 * k], places.at[2 * k])
        slot = 1 if k == 1 else 2 * k - 2
        if k == 1:
            for copy in copies[1]:
                copy.wait_recv()
        bin_source(levels, table, bins, slot, values, places, nvar)
    bin_source(levels, table, bins, 2 * ranks - 2, values, places, nvar)
    for k in range(1, ranks):
        for copy in copies[2 * k + 1]:
            copy.wait_recv()
        bin_source(levels, table, bins, 2 * k + 1, values, places, nvar)

    def add_pair(pair, carry):
        for parity in range(2):
            level = 2 * pair + parity
            rate = rate_of(band_ref[level])
            sums[level] = add_level(groups, nvar, bins, pair, parity, rate, here)
        return carry

    lax.fori_loop(0, levels // 2, add_pair, 0)

    def filter_four(quad, carry):
        for k in range(4):
            level = 4 * quad + k
            rate = rate_of(band_ref[level])
            filter_level(nvar, sums[level], filters[level], rate, fields, level)
        return carry

    lax.fori_loop(0, levels // 4, filter_four, 0)
    tap_copy.wait()

    swaps = []
    for chunk in range(levels // CHUNK):
        def correlate(k, carry, chunk=chunk):
            level = chunk * CHUNK + k
            for v in range(nvar):
                total = None
                for tap in range(TAPS):
                    other = jnp.clip(level + tap - VB, 0, levels - 1)
                    term = taps[v * levels + level, other] * fields[v, level + tap]
                    total = term if total is None else total + term
                mine[chunk, k, v] = total
            return carry

        lax.fori_loop(0, CHUNK, correlate, 0)
        swap = pltpu.make_async_remote_copy(
            src_ref=mine.at[chunk],
            dst_ref=theirs.at[chunk],
            send_sem=swap_send.at[chunk],
            recv_sem=swap_recv.at[chunk],
            device_id={"var": 1 - me},
            device_id_type=mesh_id,
        )
        swap.start()
        swaps.append(swap)
    for chunk in range(levels // CHUNK):
        swaps[chunk].wait_recv()

        def mix(k, carry, chunk=chunk):
            level = chunk * CHUNK + k
            first = [mine[chunk, k, u] for u in range(nvar)]
            second = [theirs[chunk, k, u] for u in range(nvar)]
            for v in range(nvar):
                total = None
                for u in range(nvar):
                    term = balance_ref[v, me * nvar + u] * first[u]
                    term = term + balance_ref[v, (1 - me) * nvar + u] * second[u]
                    total = term if total is None else total + term
                out_ref[v, level] = total * sigma_ref[v, level]
            return carry

        lax.fori_loop(0, CHUNK, mix, 0)
    for swap in swaps:
        swap.wait_send()
    for pair in copies.values():
        for copy in pair:
            copy.wait_send()


def on_device(innovations, obs_owner, obs_local, obs_level, band_width, vert_scale, sigma, balance):
    groups = lax.axis_size("sub")
    nvar, nobs = innovations.shape
    levels = band_width.shape[0]
    rows = BLOCKS * NX_DEV
    chunks = levels // CHUNK
    deep = nobs // LANES
    smem = pl.BlockSpec(memory_space=pltpu.SMEM)
    vmem = pl.BlockSpec(memory_space=pltpu.VMEM)
    out = pl.pallas_call(
        functools.partial(kernel, groups, levels, nvar),
        out_shape=jax.ShapeDtypeStruct((nvar, levels, rows, LANES), jnp.float32),
        in_specs=[vmem, vmem, vmem, vmem, smem, vmem, smem, smem],
        out_specs=vmem,
        scratch_shapes=[
            pltpu.VMEM((groups, nvar, nobs), jnp.float32),
            pltpu.VMEM((groups, deep, LANES), jnp.int32),
            pltpu.VMEM((deep, LANES), jnp.int32),
            pltpu.VMEM(((2 * nvar + 2) * levels // 2, 2 * LCAP), jnp.float32),
            pltpu.VMEM((groups, 2, nvar + 3, levels // 2, LCAP), jnp.float32),
            pltpu.VMEM((levels, nvar * rows, LANES), jnp.float32),
            pltpu.VMEM((levels, LANES, 2 * LANES), jnp.bfloat16),
            pltpu.VMEM((nvar, levels + 2 * VB, rows, LANES), jnp.float32),
            pltpu.VMEM((chunks, CHUNK, nvar, rows, LANES), jnp.float32),
            pltpu.VMEM((chunks, CHUNK, nvar, rows, LANES), jnp.float32),
            pltpu.VMEM((nvar * levels, 2 * levels), jnp.float32),
            pltpu.SMEM((nvar * levels, 2 * levels), jnp.float32),
            pltpu.SemaphoreType.DMA((groups,)),
            pltpu.SemaphoreType.DMA((groups,)),
            pltpu.SemaphoreType.DMA((groups,)),
            pltpu.SemaphoreType.DMA((groups,)),
            pltpu.SemaphoreType.DMA((chunks,)),
            pltpu.SemaphoreType.DMA((chunks,)),
            pltpu.SemaphoreType.DMA((3,)),
        ],
        compiler_params=pltpu.CompilerParams(
            collective_id=0, has_side_effects=True, vmem_limit_bytes=48 * 1024 * 1024
        ),
    )(
        innovations,
        obs_owner.reshape(deep, LANES),
        obs_local.reshape(deep, LANES),
        obs_level.reshape(deep, LANES),
        band_width,
        vert_scale,
        sigma,
        balance,
    )
    out = out.reshape(nvar, levels, BLOCKS, NX_DEV, LANES)
    return out.transpose(0, 1, 3, 2, 4).reshape(nvar, levels, NX_DEV, NY)


def solution(mesh):
    in_specs = (
        P("var", ("member", "sub")),
        P(("member", "sub"), None),
        P(("member", "sub")),
        P(("member", "sub"), None),
        P(),
        P("var", None),
        P("var", None),
        P("var", None),
    )
    out_specs = P("var", None, ("member", "sub"), None)
    return jax.shard_map(
        on_device, mesh=mesh, in_specs=in_specs, out_specs=out_specs, check_vma=False
    )
```

time: 400 us -> 51.9 us (0.13); the launches traced: 395 us -> 51.4 us
  other arithmetic: 135 us -> 0 us
  waiting for transfers between devices: 107 us -> 0 us
  local copies, waits for them, and re-layouts: 79.1 us -> 7.01 us
  Pallas kernels: 0 us -> 44.4 us
  starting transfers between devices: 33.7 us -> 0 us
  matrix products: 26.5 us -> 0 us
  between operations: 13.8 us -> 0.02 us
    scatter-add x3 -> x0, other arithmetic: 127 us -> none  [on_device(): column = column.at[:, spots.reshape(-1)].add(values.reshape(nvar, -1))]
    all_to_all x4 -> x0, waiting for transfers between devices: 94.9 us -> none  [the longest x1 48.3 us: on_device(): lax.all_to_all(slab, 'sub', split_axis=2, concat_axis=1, tiled=True)]
    pallas_call x0 -> x1, Pallas kernels: none -> 44.4 us  [on_device(): pl.pallas_call(functools.partial(kernel, groups, levels, nvar), out_shape...]
    reshape x3 -> x0, local copies, waits for them, and re-layouts: 41.4 us -> none  [the longest x1 35.3 us: on_device(): column = column.reshape(nvar, levels, NX_DEV, NY)]
    all_to_all x4 -> x0, starting transfers between devices: 33.7 us -> none  [the longest x1 16.3 us: on_device(): lax.all_to_all(column, 'sub', split_axis=1, concat_axis=2, tiled=True)]
    scatter x2 -> x0, local copies, waits for them, and re-layouts: 28.8 us -> none  [the longest x1 16.1 us: on_device(): spots = jnp.zeros((groups * limit,), jnp.int32).at[target].set(place)]
    dot_general x4 -> x0, matrix products: 26.5 us -> none  [the longest x1 11 us: smooth(): return jnp.einsum('vlxj,lyj->vlxy', part, along, precision=high)]
    all_gather x1 -> x0, waiting for transfers between devices: 11.8 us -> none  [on_device(): lax.all_gather(correlated, 'var', axis=0, tiled=True)]
  transfers between devices with their start and end apart: 5 -> 0, of which waited for: 4 -> 0; matrix products, arithmetic and copies ran while one was open for 6% -> 0% of each run, Pallas kernels for 0% -> 0%
where the time goes in v1:
time: 51.9 us; the launch traced here: 51.4 us
  Pallas kernels  44.4 us (86%)
  local copies, waits for them, and re-layouts  7.01 us (14%)
    pallas_call x1, Pallas kernels, on_device(): pl.pallas_call(functools.partial(kernel, groups, levels, nvar), out_shape...  44.4 us
    unnamed x17, local copies, waits for them, and re-layouts  7.01 us

profile of v1, /device:TPU:0, one launch (start us, length us, event | category | flops | bytes accessed | tf_op | source)
XLA Modules:
  0.0 51.4 jit_solution(5623085358292655060)
XLA Ops:
  0.0 0.0 copy-start
  0.0 0.8 %copy-done = f32[4,4096]{1,0:T(4,128)S(1)} copy-done((f32[4,4096]{1,0:T(4,128)S(1)}, f32[4,4096]{1,0:T(4,128)}, u32[]{:S(2)}) %copy-start) | copy-done | bytes 65560
  0.8 0.0 copy-start.1
  0.8 0.7 %copy-done.1 = s32[4096,1]{0,1:T(1,128)S(1)} copy-done((s32[4096,1]{0,1:T(1,128)S(1)}, s32[4096,1]{0,1:T(1,128)}, u32[]{:S(2)}) %copy-start.1) | copy-done | bytes 16408
  1.6 0.0 copy-start.2
  1.6 0.7 %copy-done.2 = s32[4096]{0:T(1024)S(1)} copy-done((s32[4096]{0:T(1024)S(1)}, s32[4096]{0:T(1024)}, u32[]{:S(2)}) %copy-start.2) | copy-done | bytes 16408
  2.3 0.0 copy-start.3
  2.3 0.7 %copy-done.3 = s32[4096,1]{0,1:T(1,128)S(1)} copy-done((s32[4096,1]{0,1:T(1,128)S(1)}, s32[4096,1]{0,1:T(1,128)}, u32[]{:S(2)}) %copy-start.3) | copy-done | bytes 16408
  3.0 0.0 copy-start.4
  3.0 0.7 %copy-done.4 = f32[4,64]{1,0:T(4,128)S(1)} copy-done((f32[4,64]{1,0:T(4,128)S(1)}, f32[4,64]{1,0:T(4,128)}, u32[]{:S(2)}) %copy-start.4) | copy-done | bytes 1048
  3.7 0.0 copy-start.5
  3.7 0.7 %copy-done.5 = f32[4,64]{1,0:T(4,128)S(1)} copy-done((f32[4,64]{1,0:T(4,128)S(1)}, f32[4,64]{1,0:T(4,128)}, u32[]{:S(2)}) %copy-start.5) | copy-done | bytes 1048
  4.4 0.0 copy-start.6
  4.4 0.7 %copy-done.6 = f32[4,8]{1,0:T(4,128)S(1)} copy-done((f32[4,8]{1,0:T(4,128)S(1)}, f32[4,8]{1,0:T(4,128)}, u32[]{:S(2)}) %copy-start.6) | copy-done | bytes 152
  5.0 0.0 copy-start.7
  5.0 0.7 %copy-done.7 = s32[64]{0:T(128)S(1)} copy-done((s32[64]{0:T(128)S(1)}, s32[64]{0:T(128)}, u32[]{:S(2)}) %copy-start.7) | copy-done | bytes 280
  5.7 44.4 %shard_map.82 = f32[4,64,16,128]{3,2,1,0:T(8,128)S(1)} custom-call(f32[4,4096]{1,0:T(4,128)S(1)} %copy-done, s32[32,128]{1,0:T(8,128)S(1)} %bitcast.9, s32[32,128]{1,0:T(8,128)S(1)} %bitcast.10, s32[32,128]{1,0:T(8,128)S(1)} %bitcast.11, s32[64]{0:T(128)S(1)} %copy-done.7, f32[4,64]{1,0:T(4,128)S(1)} %copy-done.4, f32[4,64]{1,0:T(4,128)S(1)} %copy-done.5, ...), custom_call_target="tpu_custom_call" | custom-call | tf_op jit(solution)/shard_map/pallas_call | solution.py:347
  50.1 1.3 %copy.11 = f32[4,64,4,512]{3,2,1,0:T(4,128)} copy(f32[4,64,4,512]{3,2,1,0:T(4,128)S(1)} %bitcast.8) | data formatting | bytes 4194304
Async XLA Ops:
  0.0 0.8 %copy-start = (f32[4,4096]{1,0:T(4,128)S(1)}, f32[4,4096]{1,0:T(4,128)}, u32[]{:S(2)}) copy-start(f32[4,4096]{1,0:T(4,128)} %value_ref.1) | copy-start | bytes 196612
  0.8 0.7 %copy-start.1 = (s32[4096,1]{0,1:T(1,128)S(1)}, s32[4096,1]{0,1:T(1,128)}, u32[]{:S(2)}) copy-start(s32[4096,1]{0,1:T(1,128)} %param.9) | copy-start | bytes 49156
  1.6 0.7 %copy-start.2 = (s32[4096]{0:T(1024)S(1)}, s32[4096]{0:T(1024)}, u32[]{:S(2)}) copy-start(s32[4096]{0:T(1024)} %param.10) | copy-start | bytes 49156
  2.3 0.7 %copy-start.3 = (s32[4096,1]{0,1:T(1,128)S(1)}, s32[4096,1]{0,1:T(1,128)}, u32[]{:S(2)}) copy-start(s32[4096,1]{0,1:T(1,128)} %param.11) | copy-start | bytes 49156
  3.0 0.7 %copy-start.4 = (f32[4,64]{1,0:T(4,128)S(1)}, f32[4,64]{1,0:T(4,128)}, u32[]{:S(2)}) copy-start(f32[4,64]{1,0:T(4,128)} %scale_ref.1) | copy-start | bytes 3076
  3.7 0.7 %copy-start.5 = (f32[4,64]{1,0:T(4,128)S(1)}, f32[4,64]{1,0:T(4,128)}, u32[]{:S(2)}) copy-start(f32[4,64]{1,0:T(4,128)} %sigma_ref.1) | copy-start | bytes 3076
  4.4 0.7 %copy-start.6 = (f32[4,8]{1,0:T(4,128)S(1)}, f32[4,8]{1,0:T(4,128)}, u32[]{:S(2)}) copy-start(f32[4,8]{1,0:T(4,128)} %balance_ref.1) | copy-start | bytes 388
  5.0 0.7 %copy-start.7 = (s32[64]{0:T(128)S(1)}, s32[64]{0:T(128)}, u32[]{:S(2)}) copy-start(s32[64]{0:T(128)} %band_ref.1) | copy-start | bytes 772

commit v2 on v1

--- a/solution.py
+++ b/solution.py
@@ -185,14 +185,28 @@
 
 
 def kernel(
-    groups, levels, nvar, value_ref, owner_ref, local_ref, level_ref, band_ref, scale_ref,
-    sigma_ref, balance_ref, out_ref, values, places, place, table, bins, sums, filters, fields,
+    groups, levels, nvar, value_hbm, owner_hbm, local_hbm, level_hbm, band_hbm, scale_hbm,
+    sigma_hbm, balance_hbm, out_ref, value_ref, owner_ref, local_ref, level_ref, band_ref,
+    scale_ref, sigma, balance, load_sem, values, places, place, table, bins, filters, fields,
     mine, theirs, taps_vmem, taps, vsend, vrecv, psend, precv, swap_send, swap_recv, own_sem,
 ):
+    loads = [
+        pltpu.make_async_copy(source, target, load_sem.at[k])
+        for k, (source, target) in enumerate(
+            [
+                (owner_hbm, owner_ref), (local_hbm, local_ref), (level_hbm, level_ref),
+                (value_hbm, value_ref), (band_hbm, band_ref), (scale_hbm, scale_ref),
+                (sigma_hbm, sigma), (balance_hbm, balance),
+            ]
+        )
+    ]
+    for load in loads:
+        load.start()
     here = lax.axis_index("sub")
     me = lax.axis_index("var")
     mesh_id = pl.DeviceIdType.MESH
     ranks = groups // 2
+    rows = BLOCKS * NX_DEV
     line, side = here // 2, lax.rem(here, 2)
     twin = 2 * line + 1 - side
     barrier = pltpu.get_barrier_semaphore()
@@ -202,6 +216,8 @@
     pl.semaphore_signal(barrier, inc=1, device_id={"var": 1 - me}, device_id_type=mesh_id)
 
     span = NX_DEV * NY
+    for load in loads:
+        load.wait()
     rank_own(levels, level_ref, owner_ref[...] * span + local_ref[...], place)
     pl.semaphore_wait(barrier, ranks + 1)
 
@@ -232,11 +248,12 @@
     bin_source(levels, table, bins, 0, values, places, nvar)
 
     eye = iota((levels, levels), 0) == iota((levels, levels), 1)
-    apart = (iota((levels, 2 * levels), 0) - iota((levels, 2 * levels), 1)).astype(jnp.float32)
+    apart = iota((levels, 2 * levels), 0) + VB - iota((levels, 2 * levels), 1)
+    apart = apart.astype(jnp.float32)
     for v in range(nvar):
         across = scale_ref[v : v + 1, :]
         down = jnp.sum(jnp.where(eye, across, 0.0), axis=1, keepdims=True)
-        across = jnp.concatenate([across, across], axis=1)
+        across = jnp.concatenate([across[:, levels - VB :], across, across[:, : levels - VB]], axis=1)
         taps_vmem[v * levels : (v + 1) * levels, :] = jnp.exp(
             -apart * apart / (2.0 * down * across)
         )
@@ -268,39 +285,41 @@
             copy.wait_recv()
         bin_source(levels, table, bins, 2 * k + 1, values, places, nvar)
 
-    def add_pair(pair, carry):
+    def smooth_pair(pair, waiting):
+        done = []
         for parity in range(2):
-            level = 2 * pair + parity
-            rate = rate_of(band_ref[level])
-            sums[level] = add_level(groups, nvar, bins, pair, parity, rate, here)
-        return carry
-
-    lax.fori_loop(0, levels // 2, add_pair, 0)
-
-    def filter_four(quad, carry):
-        for k in range(4):
-            level = 4 * quad + k
-            rate = rate_of(band_ref[level])
-            filter_level(nvar, sums[level], filters[level], rate, fields, level)
-        return carry
-
-    lax.fori_loop(0, levels // 4, filter_four, 0)
+            level = 2 * pair - 2 + parity
+            known = jnp.maximum(level, 0)
+            filter_level(
+                nvar, waiting[parity], filters[known], rate_of(band_ref[known]), fields, level
+            )
+            rate = rate_of(band_ref[2 * pair + parity])
+            done.append(add_level(groups, nvar, bins, pair, parity, rate, here))
+        return tuple(done)
+
+    empty = jnp.zeros((nvar * rows, LANES), jnp.float32)
+    last = lax.fori_loop(0, levels // 2, smooth_pair, (empty, empty))
+    for parity in range(2):
+        level = levels - 2 + parity
+        filter_level(
+            nvar, last[parity], filters[level], rate_of(band_ref[level]), fields, level
+        )
     tap_copy.wait()
 
     swaps = []
     for chunk in range(levels // CHUNK):
-        def correlate(k, carry, chunk=chunk):
-            level = chunk * CHUNK + k
-            for v in range(nvar):
-                total = None
-                for tap in range(TAPS):
-                    other = jnp.clip(level + tap - VB, 0, levels - 1)
-                    term = taps[v * levels + level, other] * fields[v, level + tap]
-                    total = term if total is None else total + term
-                mine[chunk, k, v] = total
+        def correlate(quad, carry, chunk=chunk):
+            for k in range(4):
+                level = chunk * CHUNK + quad * 4 + k
+                for v in range(nvar):
+                    total = None
+                    for tap in range(TAPS):
+                        term = taps[v * levels + level, level + tap] * fields[v, level + tap]
+                        total = term if total is None else total + term
+                    mine[chunk, quad * 4 + k, v] = total
             return carry
 
-        lax.fori_loop(0, CHUNK, correlate, 0)
+        lax.fori_loop(0, CHUNK // 4, correlate, 0)
         swap = pltpu.make_async_remote_copy(
             src_ref=mine.at[chunk],
             dst_ref=theirs.at[chunk],
@@ -314,20 +333,21 @@
     for chunk in range(levels // CHUNK):
         swaps[chunk].wait_recv()
 
-        def mix(k, carry, chunk=chunk):
-            level = chunk * CHUNK + k
-            first = [mine[chunk, k, u] for u in range(nvar)]
-            second = [theirs[chunk, k, u] for u in range(nvar)]
-            for v in range(nvar):
-                total = None
-                for u in range(nvar):
-                    term = balance_ref[v, me * nvar + u] * first[u]
-                    term = term + balance_ref[v, (1 - me) * nvar + u] * second[u]
-                    total = term if total is None else total + term
-                out_ref[v, level] = total * sigma_ref[v, level]
+        def mix(quad, carry, chunk=chunk):
+            for k in range(4):
+                level = chunk * CHUNK + quad * 4 + k
+                first = [mine[chunk, quad * 4 + k, u] for u in range(nvar)]
+                second = [theirs[chunk, quad * 4 + k, u] for u in range(nvar)]
+                for v in range(nvar):
+                    total = None
+                    for u in range(nvar):
+                        term = balance[v, me * nvar + u] * first[u]
+                        term = term + balance[v, (1 - me) * nvar + u] * second[u]
+                        total = term if total is None else total + term
+                    out_ref[v, level] = total * sigma[v, level]
             return carry
 
-        lax.fori_loop(0, CHUNK, mix, 0)
+        lax.fori_loop(0, CHUNK // 4, mix, 0)
     for swap in swaps:
         swap.wait_send()
     for pair in copies.values():
@@ -342,20 +362,28 @@
     rows = BLOCKS * NX_DEV
     chunks = levels // CHUNK
     deep = nobs // LANES
-    smem = pl.BlockSpec(memory_space=pltpu.SMEM)
+    hbm = pl.BlockSpec(memory_space=pltpu.HBM)
     vmem = pl.BlockSpec(memory_space=pltpu.VMEM)
     out = pl.pallas_call(
         functools.partial(kernel, groups, levels, nvar),
         out_shape=jax.ShapeDtypeStruct((nvar, levels, rows, LANES), jnp.float32),
-        in_specs=[vmem, vmem, vmem, vmem, smem, vmem, smem, smem],
+        in_specs=[hbm] * 8,
         out_specs=vmem,
         scratch_shapes=[
+            pltpu.VMEM((nvar, nobs), jnp.float32),
+            pltpu.VMEM((deep, LANES), jnp.int32),
+            pltpu.VMEM((deep, LANES), jnp.int32),
+            pltpu.VMEM((deep, LANES), jnp.int32),
+            pltpu.SMEM((levels,), jnp.int32),
+            pltpu.VMEM((nvar, levels), jnp.float32),
+            pltpu.SMEM((nvar, levels), jnp.float32),
+            pltpu.SMEM((nvar, 2 * nvar), jnp.float32),
+            pltpu.SemaphoreType.DMA((8,)),
             pltpu.VMEM((groups, nvar, nobs), jnp.float32),
             pltpu.VMEM((groups, deep, LANES), jnp.int32),
             pltpu.VMEM((deep, LANES), jnp.int32),
             pltpu.VMEM(((2 * nvar + 2) * levels // 2, 2 * LCAP), jnp.float32),
             pltpu.VMEM((groups, 2, nvar + 3, levels // 2, LCAP), jnp.float32),
-            pltpu.VMEM((levels, nvar * rows, LANES), jnp.float32),
             pltpu.VMEM((levels, LANES, 2 * LANES), jnp.bfloat16),
             pltpu.VMEM((nvar, levels + 2 * VB, rows, LANES), jnp.float32),
             pltpu.VMEM((chunks, CHUNK, nvar, rows, LANES), jnp.float32),
@@ -371,7 +399,7 @@
             pltpu.SemaphoreType.DMA((3,)),
         ],
         compiler_params=pltpu.CompilerParams(
-            collective_id=0, has_side_effects=True, vmem_limit_bytes=48 * 1024 * 1024
+            collective_id=0, has_side_effects=True, vmem_limit_bytes=62 * 1024 * 1024
         ),
     )(
         innovations,

time: 51.9 us -> 43.7 us (0.84)
  Pallas kernels: 44.4 us -> 40.1 us
  local copies, waits for them, and re-layouts: 7.01 us -> 3.35 us
    pallas_call x1, Pallas kernels: 44.4 us -> 40.1 us  [on_device(): pl.pallas_call(functools.partial(kernel, groups, levels, nvar), out_shape...]
    unnamed x17 -> x1, local copies, waits for them, and re-layouts: 7.01 us -> 3.35 us
where the time goes in v2:
time: 43.7 us; the launch traced here: 43.4 us
  Pallas kernels  40.1 us (92%)
  local copies, waits for them, and re-layouts  3.35 us (8%)
    pallas_call x1, Pallas kernels, on_device(): pl.pallas_call(functools.partial(kernel, groups, levels, nvar), out_shape...  40.1 us
    unnamed x1, local copies, waits for them, and re-layouts  3.35 us

profile of v2, /device:TPU:0, one launch (start us, length us, event | category | flops | bytes accessed | tf_op | source)
XLA Modules:
  0.0 43.4 jit_solution(16691281301066998912)
XLA Ops:
  0.0 40.1 %shard_map.82 = f32[4,64,16,128]{3,2,1,0:T(8,128)} custom-call(f32[4,4096]{1,0:T(4,128)} %value_hbm.1, s32[32,128]{1,0:T(8,128)} %bitcast.9, s32[32,128]{1,0:T(8,128)} %bitcast.10, s32[32,128]{1,0:T(8,128)} %bitcast.11, s32[64]{0:T(128)} %band_hbm.1, f32[4,64]{1,0:T(4,128)} %scale_hbm.1, f32[4,64]{1,0:T(4,128)} %sigma_hbm.1, f32[4,8]{1,0:T(4,128)} %balance_hbm.1), custom_call_target="tpu_custom_call" | custom-call | tf_op jit(solution)/shard_map/pallas_call | solution.py:367
  40.1 3.4 %copy.11 = f32[4,64,4,512]{3,2,1,0:T(4,128)} copy(f32[4,64,4,512]{3,2,1,0:T(4,128)} %bitcast.8) | data formatting | bytes 4194304
